TPU v7x, 32 devices: a whole 2x2x4 slice. The times are simulated.
32 devices in a mesh: dp: 16 (over z, y, x), tensor: 2 (over core).
Axes of the slice: x: 2, y: 2, z: 4, core: 2. Of those that a mesh axis runs over, the one named last changes fastest.
Arguments:
- tokens: bfloat16 [16384, 1408], P(('dp', 'tensor')), may hold values from -6 to 6
- ln1_gain: float32 [1408], replicated, may hold values from 0.1 to 1.9
- ln1_shift: float32 [1408], replicated, may hold values from -3 to 3
- w_qkv: bfloat16 [1408, 16, 264], P(None, 'tensor')
- w_out: bfloat16 [16, 88, 1408], P('tensor'), may hold values from -0.625 to 0.625
- ln2_gain: float32 [1408], replicated, may hold values from 0.1 to 1.9
- ln2_shift: float32 [1408], replicated, may hold values from -3 to 3
- w_proj: bfloat16 [5632, 3584], P('dp', 'tensor'), may hold values from -0.078125 to 0.078125
- proj_bias: float32 [3584], P('tensor'), may hold values from -3 to 3
- segments: int32 [16, 256], P('dp'), may hold values from 0 to 7, never falling along the last dimension, each value on 1 to 128 neighbouring positions
- owners: int32 [4096, 1], P('dp'), may hold values from 0 to 15; in each aligned block of 256 rows (0 to 255, 256 to 511, ...) at most 32 rows name the same one
Outputs:
- delivered: bfloat16 [8192, 3584], P('dp', 'tensor')
Inputs may be any that keep to these rules, and one draw needn't show every extreme that they name: `segments`: within a pack numbers never fall, every image has 1 to 128 groups and one has exactly that many. `owners`: among the 256 merged tokens of one pack no owner gets more than 32; in some pack an owner gets exactly 32.
All inputs are finite; a program needn't handle non-finite values.
Results may differ from a plain program's by a relative error of at most 0.015.
Values may be sent and summed in bfloat16 or wider, within the bound.
A program may use at most 128 MiB of HBM per device.

v0:
```python
import jax
import jax.numpy as jnp
from jax import lax
from jax.sharding import PartitionSpec as P


def layer_norm(values, gain, shift):
    wide = values.astype(jnp.float32)
    average = jnp.mean(wide, axis=-1, keepdims=True)
    centred = wide - average
    variance = jnp.mean(centred * centred, axis=-1, keepdims=True)
    return centred * lax.rsqrt(variance + 1e-06) * gain + shift


def attend(heads_qkv, token_segs):
    row_count = heads_qkv.shape[0]
    width = heads_qkv.shape[2] // 3
    queries = heads_qkv[:, :, :width]
    keys_all = heads_qkv[:, :, width : 2 * width]
    values_all = heads_qkv[:, :, 2 * width :]
    score_scale = 1.0 / jnp.sqrt(jnp.float32(width))
    block_rows = min(512, row_count)
    outputs = []
    for block_index in range(row_count // block_rows):
        lower = block_index * block_rows
        scores = (
            jnp.einsum(
                "qhd,khd->hqk",
                queries[lower : lower + block_rows],
                keys_all,
                preferred_element_type=jnp.float32,
            )
            * score_scale
        )
        same = token_segs[lower : lower + block_rows][:, None] == token_segs[None, :]
        scores = jnp.where(same[None], scores, -jnp.inf)
        row_max = jnp.max(scores, axis=-1, keepdims=True)
        exponent = jnp.exp(scores - row_max)
        probs = (exponent / jnp.sum(exponent, axis=-1, keepdims=True)).astype(jnp.bfloat16)
        context = jnp.einsum("hqk,khd->qhd", probs, values_all, preferred_element_type=jnp.float32)
        outputs.append(context.astype(jnp.bfloat16))
    return jnp.concatenate(outputs, axis=0)


def shards(
    tokens,
    ln1_gain,
    ln1_shift,
    w_qkv,
    w_out,
    ln2_gain,
    ln2_shift,
    w_proj,
    proj_bias,
    segments,
    owners,
):
    dp_count = lax.axis_size("dp")
    gathered = lax.all_gather(tokens, "tensor", axis=0, tiled=True)
    row_count = gathered.shape[0]
    normed = layer_norm(gathered, ln1_gain, ln1_shift).astype(jnp.bfloat16)
    heads_here = w_qkv.shape[1]
    heads_qkv = jnp.dot(
        normed, w_qkv.reshape(w_qkv.shape[0], -1), preferred_element_type=jnp.float32
    )
    heads_qkv = heads_qkv.astype(jnp.bfloat16).reshape(row_count, heads_here, -1)
    token_segs = jnp.repeat(segments[0], 4)
    context = attend(heads_qkv, token_segs).reshape(row_count, -1)
    out_flat = w_out.reshape(-1, w_out.shape[2])
    attn_all = lax.psum(
        jnp.dot(context, out_flat, preferred_element_type=jnp.float32).astype(jnp.bfloat16),
        "tensor",
    ).astype(jnp.float32)
    hidden = (gathered.astype(jnp.float32) + attn_all).astype(jnp.bfloat16)
    normed_all = layer_norm(hidden, ln2_gain, ln2_shift).astype(jnp.bfloat16)
    groups = row_count // 4
    merged = normed_all.reshape(groups, -1)
    summed = jnp.dot(
        merged, lax.all_gather(w_proj, "dp", axis=0, tiled=True), preferred_element_type=jnp.float32
    )
    projected = (summed + proj_bias).astype(jnp.bfloat16)
    dests = owners[:, 0]
    onehot = (dests[:, None] == jnp.arange(dp_count, dtype=jnp.int32)[None, :]).astype(jnp.int32)
    earlier = jnp.cumsum(onehot, axis=0) - onehot
    position = jnp.sum(earlier * onehot, axis=1)
    capacity = 2 * groups // dp_count
    slot_index = dests * capacity + position
    scatter_table = (
        slot_index[None, :] == jnp.arange(dp_count * capacity, dtype=jnp.int32)[:, None]
    ).astype(jnp.bfloat16)
    outgoing = jnp.dot(scatter_table, projected, preferred_element_type=jnp.float32).astype(
        jnp.bfloat16
    )
    outgoing = outgoing.reshape(dp_count, capacity, -1)
    arrived = lax.all_to_all(outgoing, "dp", split_axis=0, concat_axis=0, tiled=True)
    return arrived.reshape(dp_count * capacity, -1)


def solution(mesh):
    return jax.shard_map(
        shards,
        mesh=mesh,
        in_specs=(
            P(("dp", "tensor"), None),
            P(),
            P(),
            P(None, "tensor", None),
            P("tensor", None, None),
            P(),
            P(),
            P("dp", "tensor"),
            P("tensor"),
            P("dp", None),
            P("dp", None),
        ),
        out_specs=P("dp", "tensor"),
        check_vma=False,
    )
```

profile of v0, /device:TPU:0, one launch (start us, length us, event | category | flops | bytes accessed | tf_op | source)
XLA Modules:
  0.0 414.5 jit_solution(2953233517138836779)
XLA Ops:
  7.4 0.0 copy-start
  7.4 0.0 all-gather.3.cloned.1.call-start
  7.4 0.7 all-gather.3.cloned.1.call-update
  8.1 0.0 all-reduce.2.cloned.1.call-start
  8.1 0.7 slice_bitcast_fusion.1
  8.8 0.1 broadcast_in_dim.24
  8.9 0.1 eq.84
  9.0 0.1 broadcast_in_dim.28
  9.1 0.1 eq.89
  9.2 0.8 broadcast_in_dim.25
  10.0 0.1 eq.86
  10.1 0.7 broadcast_compare_fusion.1
  10.8 13.4 %all-gather.3.cloned.1.call-done = bf16[1024,1408]{1,0:T(8,128)(2,1)} async-done(((bf16[512,1408]{1,0:T(8,128)(2,1)}), bf16[1024,1408]{1,0:T(8,128)(2,1)}) %all-gather.3.cloned.1.call-update) | async-done | bytes 2883600 | tf_op jit(solution)/shard_map/all_gather | solution.py:59
  24.2 2.4 convert_reduce_fusion
  26.6 2.7 fusion.16
  29.4 0.0 copy-done.9
  29.4 0.0 copy-done.8
  29.4 0.0 copy-done.1
  29.4 9.7 %convolution_convert_fusion = bf16[1024,2112]{0,1:T(8,128)(2,1)S(1)} fusion(bf16[1408,2112]{0,1:T(8,128)(2,1)} %bitcast.51, bf16[1024,1408]{1,0:T(8,128)(2,1)S(1)} %copy-done.1, f32[1408]{0:T(1024)S(1)} %copy-done.8, f32[1408]{0:T(1024)S(1)} %copy-done.9, f32[1024]{0:T(1024)S(1)} %add_rsqrt_fusion.1, f32[1024]{0:T(1024)S(1)} %broadcast_multiply_fusion.1), kind=kOutput, calls=%fused_computation.37 | convolution fusion | flops 6100942848 | bytes 13175808 | tf_op jit(solution)/shard_map/dot_general | solution.py:63
  39.1 0.0 copy-start.4
  39.1 8.1 %fusion.40 = f32[8,512,1024]{2,1,0:T(8,128)} fusion(bf16[1024,8,264]{0,2,1:T(8,128)(2,1)S(1)} %bitcast.43), kind=kOutput, calls=%fused_computation.54 | convolution fusion | flops 738197504 | bytes 18939904 | tf_op jit(solution)/shard_map/qhd,khd->hqk/dot_general | solution.py:27
  47.2 0.0 copy-done.4
  47.2 8.1 %fusion.38 = f32[8,512,1024]{2,1,0:T(8,128)} fusion(bf16[1024,8,264]{0,2,1:T(8,128)(2,1)S(1)} %bitcast.44), kind=kOutput, calls=%fused_computation.52 | convolution fusion | flops 738197504 | bytes 18939904 | tf_op jit(solution)/shard_map/qhd,khd->hqk/dot_general | solution.py:27
  55.3 20.8 %fusion.57 = (f32[8,512]{1,0:T(8,128)S(1)}, f32[8,512,1024]{2,1,0:T(8,128)}) fusion(f32[8,512,1024]{2,1,0:T(8,128)} %fusion.40, pred[512,1024]{1,0:T(8,128)(4,1)S(1)} %get-tuple-element.5), kind=kOutput, calls=%fused_computation.86 | output fusion | flops 25166848 | bytes 34095104 | tf_op jit(solution)/shard_map/sub | solution.py:38
  76.2 7.7 %fusion.36 = bf16[512,8,88]{0,2,1:T(8,128)(2,1)S(1)} fusion(f32[8,512,1024]{2,1,0:T(8,128)} %get-tuple-element.12, f32[8,512]{1,0:T(8,128)S(1)} %get-tuple-element.11, bf16[1024,8,264]{0,2,1:T(8,128)(2,1)} %bitcast.45), kind=kOutput, calls=%fused_computation.50 | convolution fusion | flops 746946560 | bytes 18956288 | tf_op jit(solution)/shard_map/hqk,khd->qhd/dot_general | solution.py:40
  83.9 20.9 %fusion.56 = (f32[8,512]{1,0:T(8,128)S(1)}, f32[8,512,1024]{2,1,0:T(8,128)}) fusion(f32[8,512,1024]{2,1,0:T(8,128)} %fusion.38, pred[512,1024]{1,0:T(8,128)(4,1)S(1)} %get-tuple-element.6), kind=kOutput, calls=%fused_computation.85 | output fusion | flops 25166848 | bytes 34095104 | tf_op jit(solution)/shard_map/sub | solution.py:38
  104.8 7.7 %fusion.37 = bf16[512,8,88]{0,2,1:T(8,128)(2,1)S(1)} fusion(f32[8,512,1024]{2,1,0:T(8,128)} %get-tuple-element.10, f32[8,512]{1,0:T(8,128)S(1)} %get-tuple-element.9, bf16[1024,8,264]{0,2,1:T(8,128)(2,1)} %bitcast.46), kind=kOutput, calls=%fused_computation.51 | convolution fusion | flops 746946560 | bytes 18956288 | tf_op jit(solution)/shard_map/hqk,khd->qhd/dot_general | solution.py:40
  112.5 0.0 copy-start.5
  112.5 4.1 bitcast_convert_fusion
  116.6 0.0 all-reduce.2.cloned.1.call-update
  116.6 0.0 all-gather.5.cloned.1.call-start
  116.7 0.5 all-gather.5.cloned.1.call-update
  117.2 0.8 reduce-window.6
  118.1 0.2 slice_reduce_fusion
  118.3 0.1 fusion.49
  118.4 22.2 %all-reduce.2.cloned.1.call-done = bf16[1024,1408]{1,0:T(8,128)(2,1)} async-done(((bf16[1024,1408]{1,0:T(8,128)(2,1)}), bf16[1024,1408]{1,0:T(8,128)(2,1)}) %all-reduce.2.cloned.1.call-update) | async-done | bytes 2883600 | tf_op jit(solution)/shard_map/psum | solution.py:70
  140.7 3.7 convert_reduce_fusion.1
  144.3 0.8 copy-done.3
  145.1 1.2 fusion.20
  146.3 0.0 copy-start.10
  146.4 2.9 fusion.23
  149.3 5.7 %reshape.149 = bf16[256,5632]{1,0:T(8,128)(2,1)} reshape(bf16[1024,1408]{1,0:T(8,128)(2,1)} %fusion.23) | data formatting | bytes 5767168 | tf_op jit(solution)/shard_map/reshape | solution.py:77
  155.0 189.9 %all-gather.5.cloned.1.call-done = bf16[5632,1792]{1,0:T(8,128)(2,1)} async-done(((bf16[352,1792]{1,0:T(8,128)(2,1)}), bf16[5632,1792]{1,0:T(8,128)(2,1)}) %all-gather.5.cloned.1.call-update) | async-done | bytes 20185104 | tf_op jit(solution)/shard_map/all_gather | solution.py:79
  344.9 0.0 copy-done.10
  344.9 12.8 %fusion.30 = bf16[256,1792]{1,0:T(8,128)(2,1)S(1)} fusion(bf16[256,5632]{1,0:T(8,128)(2,1)} %reshape.149, bf16[5632,1792]{1,0:T(8,128)(2,1)} %all-gather.5.cloned.1.call-done, f32[1792]{0:T(1024)S(1)} %copy-done.10), kind=kOutput, calls=%fused_computation.44 | convolution fusion | flops 5168300032 | bytes 23993344 | tf_op jit(solution)/shard_map/dot_general | solution.py:78
  357.7 0.7 convolution_convert_fusion.1
  358.3 47.5 %all_to_all.5 = bf16[16,32,1792]{2,1,0:T(8,128)(2,1)S(1)} all-to-all(bf16[16,32,1792]{2,1,0:T(8,128)(2,1)S(1)} %bitcast.41), channel_id=1, replica_groups=mesh['dp'=16,'tensor'=2] {'dp'}, dimensions={0} | all-to-all | bytes 3670016 | tf_op jit(solution)/shard_map/all_to_all | solution.py:95
  405.8 1.2 copy.17
  (20 shorter events, 0.1 us)
Async XLA Ops:
  7.4 105.1 %copy-start = (bf16[8,88,1408]{2,1,0:T(8,128)(2,1)S(1)}, bf16[8,88,1408]{2,1,0:T(8,128)(2,1)}, u32[]{:S(2)}) copy-start(bf16[8,88,1408]{2,1,0:T(8,128)(2,1)} %param.15) | copy-start | bytes 5947396
  7.4 22.0 %copy-start.9 = (f32[1408]{0:T(1024)S(1)}, f32[1408]{0:T(1024)}, u32[]{:S(2)}) copy-start(f32[1408]{0:T(1024)} %param.12) | copy-start | bytes 16900
  7.4 22.0 %copy-start.8 = (f32[1408]{0:T(1024)S(1)}, f32[1408]{0:T(1024)}, u32[]{:S(2)}) copy-start(f32[1408]{0:T(1024)} %param.13) | copy-start | bytes 16900
  7.4 16.8 %all-gather.3.cloned.1.call-start = ((), (), s32[]{:S(2)}) async-start(), calls=%async_computation.1 | async-start | bytes 4325376 | tf_op jit(solution)/shard_map/all_gather | solution.py:59
  8.1 132.6 %all-reduce.2.cloned.1.call-start = ((), (), s32[]{:S(2)}) async-start(), calls=%async_computation.2 | async-start | bytes 5767168 | tf_op jit(solution)/shard_map/psum | solution.py:70
  24.2 5.2 %copy-start.1 = (bf16[1024,1408]{1,0:T(8,128)(2,1)S(1)}, bf16[1024,1408]{1,0:T(8,128)(2,1)}, u32[]{:S(2)}) copy-start(bf16[1024,1408]{1,0:T(8,128)(2,1)} %all-gather.3.cloned.1.call-done) | copy-start | bytes 8650756
  39.1 8.1 %copy-start.4 = (bf16[1024,2112]{0,1:T(8,128)(2,1)}, bf16[1024,2112]{0,1:T(8,128)(2,1)S(1)}, u32[]{:S(2)}) copy-start(bf16[1024,2112]{0,1:T(8,128)(2,1)S(1)} %convolution_convert_fusion) | copy-start | bytes 12976132
  112.5 4.7 %copy-start.5 = (s32[256,1]{0,1:T(1,128)S(1)}, s32[256,1]{0,1:T(1,128)}, u32[]{:S(2)}) copy-start(s32[256,1]{0,1:T(1,128)} %param.21) | copy-start | bytes 3076
  116.6 228.2 %all-gather.5.cloned.1.call-start = ((), (), s32[]{:S(2)}) async-start(), calls=%async_computation.3 | async-start | bytes 21446656 | tf_op jit(solution)/shard_map/all_gather | solution.py:79
  118.4 27.9 %copy-start.6 = (f32[1408]{0:T(1024)S(1)}, f32[1408]{0:T(1024)}, u32[]{:S(2)}) copy-start(f32[1408]{0:T(1024)} %param.17) | copy-start | bytes 16900
  140.7 3.7 copy-start.2
  140.7 4.5 %copy-start.3 = (bf16[1024,1408]{1,0:T(8,128)(2,1)S(1)}, bf16[1024,1408]{1,0:T(8,128)(2,1)}, u32[]{:S(2)}) copy-start(bf16[1024,1408]{1,0:T(8,128)(2,1)} %all-reduce.2.cloned.1.call-done) | copy-start | bytes 8650756
  140.7 5.7 %copy-start.7 = (f32[1408]{0:T(1024)S(1)}, f32[1408]{0:T(1024)}, u32[]{:S(2)}) copy-start(f32[1408]{0:T(1024)} %param.16) | copy-start | bytes 16900
  146.3 198.5 %copy-start.10 = (f32[1792]{0:T(1024)S(1)}, f32[1792]{0:T(1024)}, u32[]{:S(2)}) copy-start(f32[1792]{0:T(1024)} %param.19) | copy-start | bytes 21508
Sparse Core Ops, SparseCore 0:
  9.7 14.4 all-gather.2
  116.8 23.8 all-reduce.1
Sparse Core Ops, SparseCore 1:
  120.2 224.6 all-gather.4
where the time goes:
time: 415 us; the launch traced here: 414 us
  waiting for transfers between devices  227 us (55%)
  matrix products  58.9 us (14%)
  other arithmetic  56.3 us (14%)
  blocking collectives  47.5 us (11%)
  between operations  15.1 us (4%)
  local copies, waits for them, and re-layouts  9.83 us (2%)
    all_gather x1, waiting for transfers between devices, shards(): lax.all_gather(w_proj, 'dp', axis=0, tiled=True)  190 us
    all_to_all x1, blocking collectives, shards(): lax.all_to_all(outgoing, 'dp', split_axis=0, concat_axis=0, tiled=True)  47.5 us
    sub x2, other arithmetic, attend(): exponent = jnp.exp(scores - row_max)  41.7 us
    psum x1, waiting for transfers between devices, shards(): lax.psum(jnp.dot(context, out_flat, preferred_element_type=jnp.float32).a...  22.2 us
    dot_general x2, matrix products, attend(): jnp.einsum('qhd,khd->hqk', queries[lower:lower + block_rows], keys_all, p...  16.2 us
    dot_general x2, matrix products, attend(): jnp.einsum('hqk,khd->qhd', probs, values_all, preferred_element_type=jnp....  15.4 us
    all_gather x1, waiting for transfers between devices, shards(): gathered = lax.all_gather(tokens, 'tensor', axis=0, tiled=True)  13.4 us
    dot_general x1, matrix products, shards(): jnp.dot(merged, lax.all_gather(w_proj, 'dp', axis=0, tiled=True), preferr...  12.8 us
  transfers between devices with their start and end apart: 3, of which 3 were waited for; matrix products, arithmetic and copies ran while one was open for 4% of the time, Pallas kernels for 0%

commit v1 on v0

--- a/solution.py
+++ b/solution.py
@@ -1,6 +1,10 @@
+import math
+
 import jax
 import jax.numpy as jnp
 from jax import lax
+from jax.experimental import pallas as pl
+from jax.experimental.pallas import tpu as pltpu
 from jax.sharding import PartitionSpec as P
 
 
@@ -96,9 +100,254 @@
     return arrived.reshape(dp_count * capacity, -1)
 
 
+def norm_rows(wide, gain, shift):
+    average = jnp.mean(wide, axis=-1, keepdims=True)
+    centred = wide - average
+    variance = jnp.mean(centred * centred, axis=-1, keepdims=True)
+    return centred * lax.rsqrt(variance + 1e-06) * gain + shift
+
+
+def attention_kernel(
+    own_ref,
+    peer_ref,
+    gain_ref,
+    shift_ref,
+    w_ref,
+    segs_col_ref,
+    segs_row_ref,
+    w_out_ref,
+    own_term_ref,
+    peer_term_ref,
+    normed_ref,
+    context_ref,
+):
+    head = pl.program_id(0)
+    half = own_ref.shape[0]
+    rows = 2 * half
+    width = w_ref.shape[0] // 3
+    score_scale = 1.0 / math.sqrt(width)
+    step_rows = 128
+
+    @pl.when(head == 0)
+    def _():
+        for part, source in enumerate((own_ref, peer_ref)):
+
+            @pl.loop(0, half // step_rows)
+            def _(step):
+                at = pl.multiple_of(step * step_rows, step_rows)
+                wide = source[pl.ds(at, step_rows), :].astype(jnp.float32)
+                normed = norm_rows(wide, gain_ref[...], shift_ref[...])
+                to = pl.multiple_of(part * half + step * step_rows, step_rows)
+                normed_ref[pl.ds(to, step_rows), :] = normed.astype(jnp.bfloat16)
+
+    qkv = lax.dot_general(
+        w_ref[...], normed_ref[...], (((1,), (1,)), ((), ())), preferred_element_type=jnp.float32
+    )
+    queries = qkv[:width].astype(jnp.bfloat16)
+    keys = qkv[width : 2 * width].T.astype(jnp.bfloat16)
+    values = qkv[2 * width :].astype(jnp.bfloat16)
+    chunk = 256
+    for index in range(rows // chunk):
+        lanes = slice(index * chunk, (index + 1) * chunk)
+        scores = jnp.dot(keys, queries[:, lanes], preferred_element_type=jnp.float32) * score_scale
+        same = segs_col_ref[...] == segs_row_ref[:, lanes]
+        scores = jnp.where(same, scores, -jnp.inf)
+        exponent = jnp.exp(scores - jnp.max(scores, axis=0, keepdims=True))
+        total = jnp.sum(exponent, axis=0, keepdims=True)
+        summed = jnp.dot(values, exponent.astype(jnp.bfloat16), preferred_element_type=jnp.float32)
+        context_ref[pl.ds(pl.multiple_of(head * width, 8), width), lanes] = summed / total
+
+    @pl.when(head == pl.num_programs(0) - 1)
+    def _():
+        for index in range(rows // chunk):
+            lanes = slice(index * chunk, (index + 1) * chunk)
+            context = context_ref[:, lanes].T.astype(jnp.bfloat16)
+            term = jnp.dot(context, w_out_ref[...], preferred_element_type=jnp.float32)
+            target = own_term_ref if index * chunk < half else peer_term_ref
+            at = index * chunk % half
+            target[at : at + chunk, :] = term.astype(jnp.bfloat16)
+
+
+def attention_terms(own, peer, gain, shift, w_heads, segs, w_out):
+    half, depth = own.shape
+    heads, columns, _ = w_heads.shape
+    rows = 2 * half
+    whole = lambda *shape: pl.BlockSpec(shape, lambda head: (0,) * len(shape))
+    term = jax.ShapeDtypeStruct((half, depth), jnp.bfloat16)
+    return pl.pallas_call(
+        attention_kernel,
+        grid=(heads,),
+        in_specs=[
+            whole(half, depth),
+            whole(half, depth),
+            whole(1, depth),
+            whole(1, depth),
+            pl.BlockSpec((None, columns, depth), lambda head: (head, 0, 0)),
+            whole(rows, 1),
+            whole(1, rows),
+            whole(*w_out.shape),
+        ],
+        out_specs=[whole(half, depth), whole(half, depth)],
+        out_shape=[term, term],
+        scratch_shapes=[
+            pltpu.VMEM((rows, depth), jnp.bfloat16),
+            pltpu.VMEM((w_out.shape[0], rows), jnp.float32),
+        ],
+        compiler_params=pltpu.CompilerParams(vmem_limit_bytes=50 * 2**20),
+        cost_estimate=pl.CostEstimate(flops=10**9, bytes_accessed=10**6, transcendentals=0),
+    )(own, peer, gain[None], shift[None], w_heads, segs[:, None], segs[None], w_out)
+
+
+def merge_kernel(tokens_ref, here_ref, there_ref, gain_ref, shift_ref, merged_ref, normed_ref):
+    depth = tokens_ref.shape[1]
+    step_rows = 128
+
+    @pl.loop(0, tokens_ref.shape[0] // step_rows)
+    def _(step):
+        at = pl.ds(pl.multiple_of(step * step_rows, step_rows), step_rows)
+        attn = here_ref[at, :].astype(jnp.float32) + there_ref[at, :].astype(jnp.float32)
+        hidden = (tokens_ref[at, :].astype(jnp.float32) + attn).astype(jnp.bfloat16)
+        normed = norm_rows(hidden.astype(jnp.float32), gain_ref[...], shift_ref[...])
+        for piece in range(depth // 128):
+            normed_ref[piece] = normed[:, piece * 128 : (piece + 1) * 128]
+        to = pl.ds(pl.multiple_of(step * (step_rows // 4), step_rows // 4), step_rows // 4)
+        for place in range(4):
+            for piece in range(depth // 128):
+                picked = normed_ref[piece, pl.ds(place, step_rows // 4, stride=4), :]
+                lower = place * depth + piece * 128
+                merged_ref[to, lower : lower + 128] = picked.astype(jnp.bfloat16)
+
+
+def merge_tokens(tokens, here, there, gain, shift):
+    rows, depth = tokens.shape
+    return pl.pallas_call(
+        merge_kernel,
+        out_shape=jax.ShapeDtypeStruct((rows // 4, 4 * depth), jnp.bfloat16),
+        scratch_shapes=[pltpu.VMEM((depth // 128, 128, 128), jnp.float32)],
+        compiler_params=pltpu.CompilerParams(vmem_limit_bytes=32 * 2**20),
+        cost_estimate=pl.CostEstimate(flops=10**7, bytes_accessed=10**6, transcendentals=0),
+    )(tokens, here, there, gain[None], shift[None])
+
+
+def project_kernel(a_ref, b_ref, c_ref, d_ref, w_ref, bias_ref, slots_ref, side_ref, out_ref, total_ref):
+    step = pl.program_id(0)
+    rows = a_ref.shape[0]
+
+    @pl.when(step == 0)
+    def _():
+        total_ref[...] = jnp.zeros_like(total_ref)
+
+    for index, block in enumerate((a_ref, b_ref, c_ref, d_ref)):
+        total_ref[index * rows : (index + 1) * rows, :] += jnp.dot(
+            block[...], w_ref[...], preferred_element_type=jnp.float32
+        )
+
+    @pl.when(step == pl.num_programs(0) - 1)
+    def _():
+        owners_count, _, capacity, columns = out_ref.shape
+        places = lax.broadcasted_iota(jnp.int32, (owners_count * capacity, 2 * rows), 0)
+        for pack in range(2):
+            projected = total_ref[2 * pack * rows : 2 * (pack + 1) * rows, :] + bias_ref[...]
+            table = (places == slots_ref[pack : pack + 1, :]).astype(jnp.bfloat16)
+            placed = jnp.dot(
+                table, projected.astype(jnp.bfloat16), preferred_element_type=jnp.float32
+            ).astype(jnp.bfloat16)
+            out_ref[:, jnp.bitwise_xor(side_ref[0], pack)] = placed.reshape(owners_count, capacity, columns)
+
+
+def project_blocks(blocks, weights, bias, slots, side, owners_count, capacity):
+    rows, depth = blocks[0].shape
+    columns = weights.shape[1]
+    step_depth = depth // 4
+    shape = (owners_count, 2, capacity, columns)
+    block = pl.BlockSpec((rows, step_depth), lambda step: (0, step))
+    return pl.pallas_call(
+        project_kernel,
+        grid=(4,),
+        in_specs=[block] * 4
+        + [
+            pl.BlockSpec((step_depth, columns), lambda step: (step, 0)),
+            pl.BlockSpec((1, columns), lambda step: (0, 0)),
+            pl.BlockSpec(slots.shape, lambda step: (0, 0)),
+            pl.BlockSpec(memory_space=pltpu.SMEM),
+        ],
+        out_specs=pl.BlockSpec(shape, lambda step: (0, 0, 0, 0)),
+        out_shape=jax.ShapeDtypeStruct(shape, jnp.bfloat16),
+        scratch_shapes=[pltpu.VMEM((4 * rows, columns), jnp.float32)],
+        compiler_params=pltpu.CompilerParams(vmem_limit_bytes=40 * 2**20),
+        cost_estimate=pl.CostEstimate(flops=10**9, bytes_accessed=10**7, transcendentals=0),
+    )(*blocks, weights, bias, slots, side[None])
+
+
+def slot_numbers(dests, dp_count, capacity):
+    onehot = (dests[:, None] == jnp.arange(dp_count, dtype=jnp.int32)[None, :]).astype(jnp.int32)
+    earlier = jnp.cumsum(onehot, axis=0) - onehot
+    return dests * capacity + jnp.sum(earlier * onehot, axis=1)
+
+
+def paired_shards(
+    tokens,
+    ln1_gain,
+    ln1_shift,
+    w_qkv,
+    w_out,
+    ln2_gain,
+    ln2_shift,
+    w_proj,
+    proj_bias,
+    segments,
+    owners,
+):
+    dp_count = lax.axis_size("dp")
+    core = lax.axis_index("tensor")
+    side = lax.axis_index("dp") % 2
+    swap_cores = lambda array: lax.ppermute(array, "tensor", [(0, 1), (1, 0)])
+    swap_chips = lambda array: lax.ppermute(array, "dp", [(i, i ^ 1) for i in range(dp_count)])
+    columns = w_proj.shape[1] // 2
+    kept = lax.dynamic_slice_in_dim(w_proj, side * columns, columns, axis=1)
+    given = lax.dynamic_slice_in_dim(w_proj, (1 - side) * columns, columns, axis=1)
+    taken = swap_chips(given)
+    pair_rows = jnp.where(
+        side == 0,
+        jnp.concatenate([kept, taken], axis=0),
+        jnp.concatenate([taken, kept], axis=0),
+    )
+    groups_of_side = [list(range(0, dp_count, 2)), list(range(1, dp_count, 2))]
+    weights = lax.all_gather(
+        pair_rows, "dp", axis=0, tiled=True, axis_index_groups=groups_of_side
+    )
+    bias = lax.dynamic_slice_in_dim(proj_bias, side * columns, columns)[None]
+
+    other = swap_cores(tokens)
+    half = tokens.shape[0]
+    groups = 2 * half // 4
+    token_segs = jnp.repeat(jnp.roll(segments[0], -core * (groups // 2)), 4)
+    capacity = 2 * groups // dp_count
+    slots = jnp.roll(slot_numbers(owners[:, 0], dp_count, capacity), -core * (groups // 2))
+    slots = jnp.stack([slots, swap_chips(slots)])
+
+    here, there = attention_terms(
+        tokens,
+        other,
+        ln1_gain,
+        ln1_shift,
+        w_qkv.transpose(1, 2, 0),
+        token_segs,
+        w_out.reshape(-1, w_out.shape[2]),
+    )
+    merged = merge_tokens(tokens, here, swap_cores(there), ln2_gain, ln2_shift)
+    far = swap_chips(merged)
+    blocks = (merged, swap_cores(merged), far, swap_cores(far))
+    outgoing = project_blocks(blocks, weights, bias, slots, side, dp_count, capacity)
+    arrived = lax.all_to_all(outgoing, "dp", split_axis=0, concat_axis=0, tiled=True)
+    arrived = arrived.reshape(dp_count // 2, 2, 2, capacity, columns).transpose(0, 2, 3, 1, 4)
+    return arrived.reshape(dp_count * capacity, 2 * columns)
+
+
 def solution(mesh):
+    paired = mesh.shape["tensor"] == 2 and mesh.shape["dp"] == 16
     return jax.shard_map(
-        shards,
+        paired_shards if paired else shards,
         mesh=mesh,
         in_specs=(
             P(("dp", "tensor"), None),

time: 415 us -> 243 us (0.59)
  waiting for transfers between devices: 227 us -> 113 us
  matrix products: 58.9 us -> 0 us
  other arithmetic: 56.3 us -> 2.26 us
  Pallas kernels: 0 us -> 51.7 us
  starting transfers between devices: 0.09 us -> 6.82 us
    all_gather x2 -> x1, waiting for transfers between devices: 203 us -> 60.5 us  [paired_shards(): lax.all_gather(pair_rows, 'dp', axis=0, tiled=True, axis_index_groups=gro...]
    dot_general x8 -> x0, matrix products: 58.9 us -> none  [the longest x2 16.2 us: attend(): jnp.einsum('qhd,khd->hqk', queries[lower:lower + block_rows], keys_all, p...]
    ppermute x0 -> x7, waiting for transfers between devices: none -> 52.8 us  [the longest x3 47.8 us: paired_shards(): lax.ppermute(array, 'dp', [(i, i ^ 1) for i in range(dp_count)])]
    pallas_call x0 -> x3, Pallas kernels: none -> 51.7 us  [the longest x1 39.3 us: attention_terms(): pl.pallas_call(attention_kernel, grid=(heads,), in_specs=[whole(half, dep...]
    sub x2 -> x0, other arithmetic: 41.7 us -> none  [attend(): exponent = jnp.exp(scores - row_max)]
    psum x1 -> x0, waiting for transfers between devices: 22.2 us -> none  [shards(): lax.psum(jnp.dot(context, out_flat, preferred_element_type=jnp.float32).a...]
    reduce_sum x5 -> x1, other arithmetic: 10.1 us -> 0.09 us  [slot_numbers(): return dests * capacity + jnp.sum(earlier * onehot, axis=1)]
    ppermute x0 -> x7, starting transfers between devices: none -> 6.82 us  [the longest x3 6.55 us: paired_shards(): lax.ppermute(array, 'dp', [(i, i ^ 1) for i in range(dp_count)])]
  transfers between devices with their start and end apart: 3 -> 8, of which waited for: 3 -> 6; matrix products, arithmetic and copies ran while one was open for 4% -> 1% of each run, Pallas kernels for 0% -> 17%
where the time goes in v1:
time: 243 us
  waiting for transfers between devices  113 us (47%)
  Pallas kernels  51.7 us (21%)
  blocking collectives  47.5 us (20%)
  between operations  13.5 us (6%)
  local copies, waits for them, and re-layouts  7.48 us (3%)
  starting transfers between devices  6.82 us (3%)
    all_gather x1, waiting for transfers between devices, paired_shards(): lax.all_gather(pair_rows, 'dp', axis=0, tiled=True, axis_index_groups=gro...  60.5 us
    ppermute x3, waiting for transfers between devices, paired_shards(): lax.ppermute(array, 'dp', [(i, i ^ 1) for i in range(dp_count)])  47.8 us
    all_to_all x1, blocking collectives, paired_shards(): lax.all_to_all(outgoing, 'dp', split_axis=0, concat_axis=0, tiled=True)  47.5 us
    pallas_call x1, Pallas kernels, attention_terms(): pl.pallas_call(attention_kernel, grid=(heads,), in_specs=[whole(half, dep...  39.3 us
    pallas_call x1, Pallas kernels, project_blocks(): pl.pallas_call(project_kernel, grid=(4,), in_specs=[block] * 4 + [pl.Bloc...  10.5 us
    ppermute x3, starting transfers between devices, paired_shards(): lax.ppermute(array, 'dp', [(i, i ^ 1) for i in range(dp_count)])  6.55 us
    ppermute x4, waiting for transfers between devices, paired_shards(): swap_cores = lambda array: lax.ppermute(array, 'tensor', [(0, 1), (1, 0)])  4.99 us
  transfers between devices with their start and end apart: 8, of which 6 were waited for; matrix products, arithmetic and copies ran while one was open for 1% of the time, Pallas kernels for 17%

profile of v1, /device:TPU:0, one launch (start us, length us, event | category | flops | bytes accessed | tf_op | source)
XLA Modules:
  0.0 242.6 jit_solution(5613250234414239114)
XLA Ops:
  6.5 0.0 all-gather.2.cloned.1.call-start
  6.5 1.4 constant_dynamic-slice_fusion.1
  7.9 3.0 %collective-permute-start.5 = (bf16[352,896]{1,0:T(8,128)(2,1)S(1)}, bf16[352,896]{1,0:T(8,128)(2,1)S(1)}, u32[]{:S(2)}, u32[]{:S(2)}) collective-permute-start(bf16[352,896]{1,0:T(8,128)(2,1)S(1)} %get-tuple-element.11), channel_id=1, source_target_pairs={{0,2},{2,0},{4,6},{6,4},{8,10},{10,8},{12,14},{14,12},{16,18},{18,... | collective-permute-start | bytes 1892360 | tf_op jit(solution)/shard_map/ppermute | solution.py:305
  10.9 14.2 %collective-permute-done.5 = bf16[352,896]{1,0:T(8,128)(2,1)S(1)} collective-permute-done((bf16[352,896]{1,0:T(8,128)(2,1)S(1)}, bf16[352,896]{1,0:T(8,128)(2,1)S(1)}, u32[]{:S(2)}, u32[]{:S(2)}) %collective-permute-start.5) | collective-permute-done | bytes 630816 | tf_op jit(solution)/shard_map/ppermute | solution.py:305
  25.1 0.0 copy-start.8
  25.1 1.5 maximum_select_fusion
  26.6 0.0 copy-start.4
  26.6 0.0 all-gather.2.cloned.1.call-update
  26.7 0.0 copy-done
  26.7 0.1 collective-permute-start
  26.8 0.0 copy-done.8
  26.8 0.1 dynamic_slice.16
  26.9 0.1 broadcast_in_dim.24
  27.0 0.1 broadcast_in_dim_reshape.7.segs_row_ref
  27.1 0.2 broadcast_in_dim_reshape.8.segs_col_ref
  27.3 0.0 copy-done.4
  27.3 0.7 broadcast_in_dim.23.shift_ref
  28.0 1.9 collective-permute-done.peer_ref
  30.0 0.0 copy-start.2
  30.0 1.1 copy-done.2
  31.1 0.0 copy-start.5
  31.1 39.3 %shard_map.109 = (bf16[512,1408]{1,0:T(8,128)(2,1)S(1)}, bf16[512,1408]{1,0:T(8,128)(2,1)S(1)}) custom-call(bf16[512,1408]{1,0:T(8,128)(2,1)} %tokens_ref.1, bf16[512,1408]{1,0:T(8,128)(2,1)} %copy-done.2, f32[1,1408]{1,0:T(1,128)S(1)} %broadcast_in_dim.22.gain_ref, f32[1,1408]{1,0:T(1,128)S(1)} %broadcast_in_dim.23.shift_ref, ...), custom_call_target="tpu_custom_call" | custom-call | flops 1000000000 | bytes 1000000 | tf_op jit(solution)/shard_map/pallas_call | solution.py:177
  70.3 0.2 collective-permute-start.1
  70.5 0.0 copy-done.5
  70.5 0.0 copy-done.6
  70.6 3.1 %collective-permute-done.1.there_ref = bf16[512,1408]{1,0:T(8,128)(2,1)S(1)} collective-permute-done((bf16[512,1408]{1,0:T(8,128)(2,1)S(1)}, bf16[512,1408]{1,0:T(8,128)(2,1)S(1)}, u32[]{:S(2)}, u32[]{:S(2)}) %collective-permute-start.1) | collective-permute-done | bytes 1441824 | tf_op jit(solution)/shard_map/ppermute | solution.py:304
  73.6 0.0 copy-done.1
  73.6 1.9 shard_map.110.a_ref
  75.5 1.8 collective-permute-start.3
  77.3 0.0 collective-permute-start.2
  77.4 31.9 %collective-permute-done.3.c_ref = bf16[128,5632]{1,0:T(8,128)(2,1)S(1)} collective-permute-done((bf16[128,5632]{1,0:T(8,128)(2,1)S(1)}, bf16[128,5632]{1,0:T(8,128)(2,1)S(1)}, u32[]{:S(2)}, u32[]{:S(2)}) %collective-permute-start.3) | collective-permute-done | bytes 1441824 | tf_op jit(solution)/shard_map/ppermute | solution.py:305
  109.2 0.0 collective-permute-start.4
  109.3 0.0 copy-done.3
  109.3 0.6 reduce-window.6
  109.9 0.2 slice_reduce_fusion
  110.1 0.1 fusion.2
  110.2 0.1 dynamic_slice.17
  110.3 1.7 collective-permute-start.6
  112.0 0.0 copy-done.7
  112.0 0.1 dynamic_slice.14
  112.1 1.7 collective-permute-done.6
  113.9 0.0 collective-permute-done.2.b_ref
  113.9 0.0 collective-permute-done.4.d_ref
  113.9 60.5 %all-gather.2.cloned.1.call-done.w_ref = bf16[5632,896]{1,0:T(8,128)(2,1)} async-done(((bf16[704,896]{1,0:T(8,128)(2,1)}), bf16[5632,896]{1,0:T(8,128)(2,1)}) %all-gather.2.cloned.1.call-update) | async-done | bytes 10092560 | tf_op jit(solution)/shard_map/all_gather | solution.py:316
  174.4 10.5 %shard_map.111 = bf16[16,2,32,896]{3,2,1,0:T(8,128)(2,1)S(1)} custom-call(bf16[128,5632]{1,0:T(8,128)(2,1)S(1)} %shard_map.110.a_ref, bf16[128,5632]{1,0:T(8,128)(2,1)} %collective-permute-done.2.b_ref, bf16[128,5632]{1,0:T(8,128)(2,1)S(1)} %collective-permute-done.3.c_ref, bf16[128,5632]{1,0:T(8,128)(2,1)} %collective-permute-done.4.d_ref, ...), custom_call_target="tpu_custom_call" | custom-call | flops 1000000000 | bytes 10000000 | tf_op jit(solution)/shard_map/pallas_call | solution.py:264
  184.9 47.5 %all_to_all.5 = bf16[16,2,32,896]{3,2,1,0:T(8,128)(2,1)S(1)} all-to-all(bf16[16,2,32,896]{3,2,1,0:T(8,128)(2,1)S(1)} %shard_map.111), channel_id=1, replica_groups=mesh['dp'=16,'tensor'=2] {'dp'}, dimensions={0} | all-to-all | bytes 3670016 | tf_op jit(solution)/shard_map/all_to_all | solution.py:342
  232.3 1.9 copy.15
  234.2 1.5 copy.17
  (16 shorter events, 0.1 us)
Async XLA Ops:
  6.5 167.8 %all-gather.2.cloned.1.call-start = ((), (), s32[]{:S(2)}) async-start(), calls=%async_computation.1 | async-start | bytes 11354112 | tf_op jit(solution)/shard_map/all_gather | solution.py:316
  7.9 17.2 %collective-permute-start.5 = (bf16[352,896]{1,0:T(8,128)(2,1)S(1)}, bf16[352,896]{1,0:T(8,128)(2,1)S(1)}, u32[]{:S(2)}, u32[]{:S(2)}) collective-permute-start(bf16[352,896]{1,0:T(8,128)(2,1)S(1)} %get-tuple-element.11), channel_id=1, source_target_pairs={{0,2},{2,0},{4,6},{6,4},{8,10},{10,8},{12,14},{14,12},{16,18},{18,... | collective-permute-start | bytes 1892360 | tf_op jit(solution)/shard_map/ppermute | solution.py:305
  25.1 1.5 copy-start
  25.1 1.6 copy-start.8
  26.6 0.7 copy-start.4
  26.7 3.3 %collective-permute-start = (bf16[512,1408]{1,0:T(8,128)(2,1)S(1)}, bf16[512,1408]{1,0:T(8,128)(2,1)S(1)}, u32[]{:S(2)}, u32[]{:S(2)}) collective-permute-start(bf16[512,1408]{1,0:T(8,128)(2,1)S(1)} %copy-done), channel_id=1, source_target_pairs={{0,1},{1,0},{2,3},{3,2},{4,5},{5,4},{6,7},{7,6},{8,9},{9,8},{10,11... | collective-permute-start | bytes 4325384 | tf_op jit(solution)/shard_map/ppermute | solution.py:304
  30.0 1.1 copy-start.2
  31.1 39.5 %copy-start.5 = (f32[1408]{0:T(1024)S(1)}, f32[1408]{0:T(1024)}, u32[]{:S(2)}) copy-start(f32[1408]{0:T(1024)} %param.18) | copy-start | bytes 16900
  31.1 39.5 %copy-start.6 = (f32[1408]{0:T(1024)S(1)}, f32[1408]{0:T(1024)}, u32[]{:S(2)}) copy-start(f32[1408]{0:T(1024)} %param.19) | copy-start | bytes 16900
  31.1 42.6 %copy-start.1 = (bf16[512,1408]{1,0:T(8,128)(2,1)S(1)}, bf16[512,1408]{1,0:T(8,128)(2,1)}, u32[]{:S(2)}) copy-start(bf16[512,1408]{1,0:T(8,128)(2,1)} %tokens_ref.1) | copy-start | bytes 4325380
  70.3 3.3 %collective-permute-start.1 = (bf16[512,1408]{1,0:T(8,128)(2,1)S(1)}, bf16[512,1408]{1,0:T(8,128)(2,1)S(1)}, u32[]{:S(2)}, u32[]{:S(2)}) collective-permute-start(bf16[512,1408]{1,0:T(8,128)(2,1)S(1)} %get-tuple-element.9), channel_id=1, source_target_pairs={{0,1},{1,0},{2,3},{3,2},{4,5},{5,4},{6,7},{7,6},{8,9},{9,8},{10,11... | collective-permute-start | bytes 4325384 | tf_op jit(solution)/shard_map/ppermute | solution.py:304
  73.6 35.6 %copy-start.3 = (s32[256,1]{0,1:T(1,128)S(1)}, s32[256,1]{0,1:T(1,128)}, u32[]{:S(2)}) copy-start(s32[256,1]{0,1:T(1,128)} %param.23) | copy-start | bytes 3076
  73.6 38.4 %copy-start.7 = (f32[1792]{0:T(1024)S(1)}, f32[1792]{0:T(1024)}, u32[]{:S(2)}) copy-start(f32[1792]{0:T(1024)} %param.21) | copy-start | bytes 21508
  75.5 33.7 %collective-permute-start.3 = (bf16[128,5632]{1,0:T(8,128)(2,1)S(1)}, bf16[128,5632]{1,0:T(8,128)(2,1)S(1)}, u32[]{:S(2)}, u32[]{:S(2)}) collective-permute-start(bf16[128,5632]{1,0:T(8,128)(2,1)S(1)} %shard_map.110.a_ref), channel_id=1, source_target_pairs={{0,2},{2,0},{4,6},{6,4},{8,10},{10,8},{12,14},{14,12},{16,18},{18,... | collective-permute-start | bytes 4325384 | tf_op jit(solution)/shard_map/ppermute | solution.py:305
  77.3 36.5 %collective-permute-start.2 = (bf16[128,5632]{1,0:T(8,128)(2,1)S(1)}, bf16[128,5632]{1,0:T(8,128)(2,1)}, u32[]{:S(2)}, u32[]{:S(2)}) collective-permute-start(bf16[128,5632]{1,0:T(8,128)(2,1)S(1)} %shard_map.110.a_ref), channel_id=1, source_target_pairs={{0,1},{1,0},{2,3},{3,2},{4,5},{5,4},{6,7},{7,6},{8,9},{9,8},{10,11... | collective-permute-start | bytes 4325384 | tf_op jit(solution)/shard_map/ppermute | solution.py:304
  109.2 4.6 %collective-permute-start.4 = (bf16[128,5632]{1,0:T(8,128)(2,1)S(1)}, bf16[128,5632]{1,0:T(8,128)(2,1)}, u32[]{:S(2)}, u32[]{:S(2)}) collective-permute-start(bf16[128,5632]{1,0:T(8,128)(2,1)S(1)} %collective-permute-done.3.c_ref), channel_id=1, source_target_pairs={{0,1},{1,0},{2,3},{3,2},{4,5},{5,4},{6,7},{7,6},{8,9},{9,8},{10,11... | collective-permute-start | bytes 4325384 | tf_op jit(solution)/shard_map/ppermute | solution.py:304
  110.3 3.6 %collective-permute-start.6 = (s32[256]{0:T(256)S(1)}, s32[256]{0:T(256)S(1)}, u32[]{:S(2)}, u32[]{:S(2)}) collective-permute-start(s32[256]{0:T(256)S(1)} %dynamic_slice.17), channel_id=1, source_target_pairs={{0,2},{2,0},{4,6},{6,4},{8,10},{10,8},{12,14},{14,12},{16,18},{18,... | collective-permute-start | bytes 3080 | tf_op jit(solution)/shard_map/ppermute | solution.py:305
Sparse Core Ops, SparseCore 0:
  26.8 147.5 all-gather.1

commit v2 on v0

--- a/solution.py
+++ b/solution.py
@@ -1,6 +1,10 @@
+import math
+
 import jax
 import jax.numpy as jnp
 from jax import lax
+from jax.experimental import pallas as pl
+from jax.experimental.pallas import tpu as pltpu
 from jax.sharding import PartitionSpec as P
 
 
@@ -96,9 +100,331 @@
     return arrived.reshape(dp_count * capacity, -1)
 
 
+def norm_rows(wide, gain, shift):
+    average = jnp.mean(wide, axis=-1, keepdims=True)
+    centred = wide - average
+    variance = jnp.mean(centred * centred, axis=-1, keepdims=True)
+    return centred * lax.rsqrt(variance + 1e-06) * gain + shift
+
+
+MESH = pl.DeviceIdType.MESH
+FIRST_SENDS = ((0, 4), (0, 1), (0, 2), (0, 8))
+AFTER_PAIR = ((4, 8), (4, 2), (4, 1))
+AFTER_NEAR = ((1, 2), (8, 1), (8, 2))
+ALL_SENDS = FIRST_SENDS + AFTER_PAIR + AFTER_NEAR + ((6, 1), (12, 2), (12, 1), (9, 2), (14, 1))
+
+
+def flipped(index, offset):
+    result = index
+    for bit in range(4):
+        if offset >> bit & 1:
+            result = result + (1 << bit) * (1 - 2 * (index // (1 << bit) % 2))
+    return result
+
+
+def sublayer_kernel(
+    own_ref,
+    gain1_ref,
+    shift1_ref,
+    w_ref,
+    segs_col_ref,
+    segs_row_ref,
+    w_out_ref,
+    gain2_ref,
+    shift2_ref,
+    w_proj_ref,
+    bias_ref,
+    slots_ref,
+    out_ref,
+    peer_ref,
+    normed_ref,
+    context_ref,
+    here_ref,
+    there_ref,
+    arrived_ref,
+    pieces_ref,
+    blocks_ref,
+    gathered_ref,
+    total_ref,
+    far_slots_ref,
+    send_sems,
+    recv_sems,
+):
+    dp, core = lax.axis_index("dp"), lax.axis_index("tensor")
+    half, depth = own_ref.shape
+    rows = 2 * half
+    width = w_ref.shape[1] // 3
+    columns = gathered_ref.shape[2]
+    score_scale = 1.0 / math.sqrt(width)
+    parity = dp // 4 % 2
+    beside = (dp, 1 - core)
+    facing = (flipped(dp, 4), core)
+
+    def remote(source, target, number, device):
+        return pltpu.make_async_remote_copy(
+            src_ref=source,
+            dst_ref=target,
+            send_sem=send_sems.at[number],
+            recv_sem=recv_sems.at[number],
+            device_id=device,
+            device_id_type=MESH,
+        )
+
+    def lanes_of(side):
+        return pl.ds(pl.multiple_of(side * columns, 128), columns)
+
+    def shard_copy(shard, partner):
+        index = flipped(dp, shard)
+        if shard == 0:
+            side = 1 - parity if partner == 4 else parity
+            source = w_proj_ref.at[:, lanes_of(side)]
+        else:
+            source = gathered_ref.at[index]
+        return remote(source, gathered_ref.at[index], shard ^ partner, (flipped(dp, partner), core))
+
+    def wait_shard(offset):
+        place = gathered_ref.at[flipped(dp, offset)]
+        remote(place, place, offset, facing).wait_recv()
+
+    barrier = pltpu.get_barrier_semaphore()
+    for device in [(flipped(dp, bit), core) for bit in (1, 2, 4, 8)] + [beside]:
+        pl.semaphore_signal(barrier, inc=1, device_id=device, device_id_type=MESH)
+    pl.semaphore_wait(barrier, 5)
+
+    token_copy = remote(own_ref, peer_ref, 16, beside)
+    token_copy.start()
+    for send in FIRST_SENDS:
+        shard_copy(*send).start()
+    slots_copy = remote(slots_ref, far_slots_ref, 21, facing)
+    slots_copy.start()
+    own_copy = pltpu.make_async_copy(
+        w_proj_ref.at[:, lanes_of(parity)], gathered_ref.at[dp], recv_sems.at[0]
+    )
+    own_copy.start()
+
+    step_rows = 128
+
+    def first_norm(part, source):
+        @pl.loop(0, half // step_rows)
+        def _(step):
+            at = pl.multiple_of(step * step_rows, step_rows)
+            wide = source[pl.ds(at, step_rows), :].astype(jnp.float32)
+            normed = norm_rows(wide, gain1_ref[...], shift1_ref[...])
+            to = pl.multiple_of(part * half + step * step_rows, step_rows)
+            normed_ref[pl.ds(to, step_rows), :] = normed.astype(jnp.bfloat16)
+
+    first_norm(0, own_ref)
+    token_copy.wait_recv()
+    first_norm(1, peer_ref)
+
+    chunk = 256
+
+    def heads(first, last):
+        @pl.loop(first, last)
+        def _(head):
+            qkv = lax.dot_general(
+                w_ref[head],
+                normed_ref[...],
+                (((1,), (1,)), ((), ())),
+                preferred_element_type=jnp.float32,
+            )
+            queries = qkv[:width].astype(jnp.bfloat16)
+            keys = qkv[width : 2 * width].T.astype(jnp.bfloat16)
+            values = qkv[2 * width :].astype(jnp.bfloat16)
+            for index in range(rows // chunk):
+                lanes = slice(index * chunk, (index + 1) * chunk)
+                scores = jnp.dot(keys, queries[:, lanes], preferred_element_type=jnp.float32)
+                same = segs_col_ref[...] == segs_row_ref[:, lanes]
+                scores = jnp.where(same, scores * score_scale, -jnp.inf)
+                exponent = jnp.exp(scores - jnp.max(scores, axis=0, keepdims=True))
+                total = jnp.sum(exponent, axis=0, keepdims=True)
+                summed = jnp.dot(
+                    values, exponent.astype(jnp.bfloat16), preferred_element_type=jnp.float32
+                )
+                context_ref[head, :, lanes] = summed / total
+
+    heads(0, 3)
+    wait_shard(4)
+    for send in AFTER_PAIR:
+        shard_copy(*send).start()
+    heads(3, 6)
+    wait_shard(1)
+    wait_shard(8)
+    for send in AFTER_NEAR:
+        shard_copy(*send).start()
+    heads(6, w_ref.shape[0])
+    wait_shard(6)
+    shard_copy(6, 1).start()
+
+    def terms(first, target):
+        for index in range(half // chunk):
+            lanes = slice(first + index * chunk, first + (index + 1) * chunk)
+            context = context_ref[:, :, lanes].reshape(-1, chunk).T.astype(jnp.bfloat16)
+            term = jnp.dot(context, w_out_ref[...], preferred_element_type=jnp.float32)
+            target[index * chunk : (index + 1) * chunk, :] = term.astype(jnp.bfloat16)
+
+    terms(half, there_ref)
+    term_copy = remote(there_ref, arrived_ref, 17, beside)
+    term_copy.start()
+    terms(0, here_ref)
+    term_copy.wait_recv()
+
+    @pl.loop(0, half // step_rows)
+    def _(step):
+        at = pl.ds(pl.multiple_of(step * step_rows, step_rows), step_rows)
+        attn = here_ref[at, :].astype(jnp.float32) + arrived_ref[at, :].astype(jnp.float32)
+        hidden = (own_ref[at, :].astype(jnp.float32) + attn).astype(jnp.bfloat16)
+        normed = norm_rows(hidden.astype(jnp.float32), gain2_ref[...], shift2_ref[...])
+        for piece in range(depth // 128):
+            pieces_ref[piece] = normed[:, piece * 128 : (piece + 1) * 128]
+        quarter = step_rows // 4
+        to = pl.ds(pl.multiple_of(step * quarter, quarter), quarter)
+        for place in range(4):
+            for piece in range(depth // 128):
+                picked = pieces_ref[piece, pl.ds(place, quarter, stride=4), :]
+                lanes = slice(piece * 128, (piece + 1) * 128)
+                blocks_ref[0, place, to, lanes] = picked.astype(jnp.bfloat16)
+
+    far_copy = remote(blocks_ref.at[0], blocks_ref.at[2], 18, facing)
+    far_copy.start()
+    near_copy = remote(blocks_ref.at[0], blocks_ref.at[1], 19, beside)
+    near_copy.start()
+
+    block_rows = blocks_ref.shape[2]
+
+    def project(offset, first, fresh):
+        place = flipped(dp, offset) // 4
+        weights = gathered_ref[pl.ds(4 * place, 4)].reshape(-1, columns)
+        for block in (first, first + 1):
+            at = slice(block * block_rows, (block + 1) * block_rows)
+            product = jnp.dot(blocks_ref[block, place], weights, preferred_element_type=jnp.float32)
+            total_ref[at, :] = product if fresh else total_ref[at, :] + product
+
+    wait_shard(12)
+    shard_copy(12, 2).start()
+    shard_copy(12, 1).start()
+    wait_shard(9)
+    shard_copy(9, 2).start()
+    near_copy.wait_recv()
+    own_copy.wait()
+    wait_shard(2)
+    wait_shard(3)
+    project(0, 0, True)
+    wait_shard(14)
+    shard_copy(14, 1).start()
+    far_copy.wait_recv()
+    across_copy = remote(blocks_ref.at[2], blocks_ref.at[3], 20, beside)
+    across_copy.start()
+    wait_shard(5)
+    wait_shard(7)
+    project(4, 0, False)
+    across_copy.wait_recv()
+    project(0, 2, True)
+    project(4, 2, False)
+    wait_shard(10)
+    wait_shard(11)
+    project(8, 0, False)
+    project(8, 2, False)
+    wait_shard(13)
+    wait_shard(15)
+    project(12, 0, False)
+    project(12, 2, False)
+    slots_copy.wait_recv()
+
+    dp_count, _, capacity, _ = out_ref.shape
+    places = lax.broadcasted_iota(jnp.int32, (dp_count * capacity, 2 * block_rows), 0)
+    for pack, slots in enumerate((slots_ref, far_slots_ref)):
+        at = slice(2 * pack * block_rows, 2 * (pack + 1) * block_rows)
+        projected = (total_ref[at, :] + bias_ref[...]).astype(jnp.bfloat16)
+        table = (places == slots[...]).astype(jnp.bfloat16)
+        placed = jnp.dot(table, projected, preferred_element_type=jnp.float32)
+        slot = parity if pack == 0 else 1 - parity
+        out_ref[:, slot] = placed.astype(jnp.bfloat16).reshape(dp_count, capacity, columns)
+
+    for send in ALL_SENDS:
+        shard_copy(*send).wait_send()
+    for copy in (token_copy, slots_copy, term_copy, far_copy, near_copy, across_copy):
+        copy.wait_send()
+
+
+def slot_numbers(dests, dp_count, capacity):
+    onehot = (dests[:, None] == jnp.arange(dp_count, dtype=jnp.int32)[None, :]).astype(jnp.int32)
+    earlier = jnp.cumsum(onehot, axis=0) - onehot
+    return dests * capacity + jnp.sum(earlier * onehot, axis=1)
+
+
+def paired_shards(
+    tokens,
+    ln1_gain,
+    ln1_shift,
+    w_qkv,
+    w_out,
+    ln2_gain,
+    ln2_shift,
+    w_proj,
+    proj_bias,
+    segments,
+    owners,
+):
+    dp_count = lax.axis_size("dp")
+    core = lax.axis_index("tensor")
+    parity = lax.axis_index("dp") // 4 % 2
+    columns = w_proj.shape[1] // 2
+    half, depth = tokens.shape
+    groups = 2 * half // 4
+    capacity = 2 * groups // dp_count
+    bias = lax.dynamic_slice_in_dim(proj_bias, parity * columns, columns)
+    token_segs = jnp.repeat(jnp.roll(segments[0], -core * (groups // 2)), 4)
+    slots = jnp.roll(slot_numbers(owners[:, 0], dp_count, capacity), -core * (groups // 2))
+    heads_here, width, _ = w_out.shape
+    half_rows = pltpu.VMEM((half, depth), jnp.bfloat16)
+    outgoing = pl.pallas_call(
+        sublayer_kernel,
+        in_specs=[pl.BlockSpec(memory_space=pltpu.VMEM)] * 12,
+        out_specs=pl.BlockSpec(memory_space=pltpu.VMEM),
+        out_shape=jax.ShapeDtypeStruct((dp_count, 2, capacity, columns), jnp.bfloat16),
+        scratch_shapes=[
+            half_rows,
+            pltpu.VMEM((2 * half, depth), jnp.bfloat16),
+            pltpu.VMEM((heads_here, width, 2 * half), jnp.float32),
+            half_rows,
+            half_rows,
+            half_rows,
+            pltpu.VMEM((depth // 128, 128, 128), jnp.float32),
+            pltpu.VMEM((4, 4, half // 4, depth), jnp.bfloat16),
+            pltpu.VMEM((dp_count, w_proj.shape[0], columns), jnp.bfloat16),
+            pltpu.VMEM((half, columns), jnp.float32),
+            pltpu.VMEM((1, groups), jnp.int32),
+            pltpu.SemaphoreType.DMA((22,)),
+            pltpu.SemaphoreType.DMA((22,)),
+        ],
+        compiler_params=pltpu.CompilerParams(
+            collective_id=0, has_side_effects=True, vmem_limit_bytes=60 * 2**20
+        ),
+        cost_estimate=pl.CostEstimate(flops=10**10, bytes_accessed=10**7, transcendentals=0),
+    )(
+        tokens,
+        ln1_gain[None],
+        ln1_shift[None],
+        w_qkv.transpose(1, 2, 0),
+        token_segs[:, None],
+        token_segs[None],
+        w_out.reshape(-1, depth),
+        ln2_gain[None],
+        ln2_shift[None],
+        w_proj,
+        bias[None],
+        slots[None],
+    )
+    arrived = lax.all_to_all(outgoing, "dp", split_axis=0, concat_axis=0, tiled=True)
+    arrived = arrived.reshape(dp_count // 8, 2, 4, 2, capacity, columns)
+    return arrived.transpose(0, 3, 2, 4, 1, 5).reshape(dp_count * capacity, 2 * columns)
+
+
 def solution(mesh):
+    paired = mesh.shape["tensor"] == 2 and mesh.shape["dp"] == 16
     return jax.shard_map(
-        shards,
+        paired_shards if paired else shards,
         mesh=mesh,
         in_specs=(
             P(("dp", "tensor"), None),

time: 415 us -> 177 us (0.43)
  waiting for transfers between devices: 227 us -> 0 us
  Pallas kernels: 0 us -> 113 us
  matrix products: 58.9 us -> 0 us
  other arithmetic: 56.3 us -> 3.52 us
  between operations: 15.1 us -> 0.03 us
    all_gather x2 -> x0, waiting for transfers between devices: 203 us -> none  [the longest x1 190 us: shards(): lax.all_gather(w_proj, 'dp', axis=0, tiled=True)]
    pallas_call x0 -> x1, Pallas kernels: none -> 113 us  [paired_shards(): pl.pallas_call(sublayer_kernel, in_specs=[pl.BlockSpec(memory_space=pltpu...]
    dot_general x8 -> x0, matrix products: 58.9 us -> none  [the longest x2 16.2 us: attend(): jnp.einsum('qhd,khd->hqk', queries[lower:lower + block_rows], keys_all, p...]
    sub x2 -> x0, other arithmetic: 41.7 us -> none  [attend(): exponent = jnp.exp(scores - row_max)]
    psum x1 -> x0, waiting for transfers between devices: 22.2 us -> none  [shards(): lax.psum(jnp.dot(context, out_flat, preferred_element_type=jnp.float32).a...]
    reduce_sum x5 -> x1, other arithmetic: 10.1 us -> 0.77 us  [slot_numbers(): return dests * capacity + jnp.sum(earlier * onehot, axis=1)]
    reshape x1 -> x0, local copies, waits for them, and re-layouts: 5.66 us -> none  [shards(): merged = normed_all.reshape(groups, -1)]
    broadcast_in_dim x3 -> x6, local copies, waits for them, and re-layouts: 0.92 us -> 5.85 us  [the longest x1 1.3 us: paired_shards(): ln1_shift[None]]
  transfers between devices with their start and end apart: 3 -> 0, of which waited for: 3 -> 0; matrix products, arithmetic and copies ran while one was open for 4% -> 0% of each run, Pallas kernels for 0% -> 0%
where the time goes in v2:
time: 177 us
  Pallas kernels  113 us (64%)
  blocking collectives  47.3 us (27%)
  local copies, waits for them, and re-layouts  12.6 us (7%)
  other arithmetic  3.52 us (2%)
    pallas_call x1, Pallas kernels, paired_shards(): pl.pallas_call(sublayer_kernel, in_specs=[pl.BlockSpec(memory_space=pltpu...  113 us
    all_to_all x1, blocking collectives, paired_shards(): lax.all_to_all(outgoing, 'dp', split_axis=0, concat_axis=0, tiled=True)  47.3 us

profile of v2, /device:TPU:0, one launch (start us, length us, event | category | flops | bytes accessed | tf_op | source)
XLA Modules:
  0.0 176.9 jit_solution(5020996495795895173)
XLA Ops:
  0.0 0.8 pad_add_fusion
  0.8 0.1 dynamic_slice.8
  0.8 0.1 broadcast_in_dim.24
  0.9 0.7 broadcast_in_dim_reshape.7.segs_row_ref
  1.7 1.0 broadcast_in_dim_reshape.8.segs_col_ref
  2.6 0.8 dynamic_slice.6
  3.4 0.6 broadcast_in_dim.27.bias_ref
  4.0 1.3 broadcast_in_dim.22.gain1_ref
  5.3 1.3 broadcast_in_dim.23.shift1_ref
  6.6 1.3 broadcast_in_dim.25.gain2_ref
  7.9 1.3 broadcast_in_dim.26.shift2_ref
  9.2 0.7 fusion.3
  9.8 0.6 reduce-window.6
  10.4 0.2 slice_reduce_fusion
  10.6 0.8 fusion.2
  11.4 0.7 multiply_add_fusion
  12.1 0.6 dynamic_slice.9
  12.8 113.4 %shard_map.109 = bf16[16,2,32,896]{3,2,1,0:T(8,128)(2,1)} custom-call(bf16[512,1408]{1,0:T(8,128)(2,1)} %own_ref.1, f32[1,1408]{1,0:T(1,128)} %broadcast_in_dim.22.gain1_ref, f32[1,1408]{1,0:T(1,128)} %broadcast_in_dim.23.shift1_ref, bf16[8,264,1408]{2,1,0:T(8,128)(2,1)} %bitcast.38, s32[1024,1]{1,0:T(8,128)} %broadcast_in_dim_reshape.8.segs_col_ref, ...), custom_call_target="tpu_custom_call" | custom-call | flops 10000000000 | bytes 10000000 | tf_op jit(solution)/shard_map/pallas_call | solution.py:381
  126.2 47.3 %all_to_all.5 = bf16[16,2,32,896]{3,2,1,0:T(8,128)(2,1)S(1)} all-to-all(bf16[16,2,32,896]{3,2,1,0:T(8,128)(2,1)} %shard_map.109), channel_id=1, replica_groups=mesh['dp'=16,'tensor'=2] {'dp'}, dimensions={0} | all-to-all | bytes 3670016 | tf_op jit(solution)/shard_map/all_to_all | solution.py:419
  173.5 1.9 %copy.15 = bf16[2,2,4,32,2,896]{5,4,3,2,1,0:T(2,128)(2,1)S(1)} copy(bf16[2,2,4,32,2,896]{5,3,1,2,4,0:T(8,128)(2,1)S(1)} %bitcast.31) | data formatting | bytes 3670016 | tf_op jit(solution)/shard_map/transpose | solution.py:421
  175.4 1.5 copy.17
  (3 shorter events, 0.1 us)

commit v3 on v2

--- a/solution.py
+++ b/solution.py
@@ -110,8 +110,8 @@
 MESH = pl.DeviceIdType.MESH
 FIRST_SENDS = ((0, 4), (0, 1), (0, 2), (0, 8))
 AFTER_PAIR = ((4, 8), (4, 2), (4, 1))
-AFTER_NEAR = ((1, 2), (8, 1), (8, 2))
-ALL_SENDS = FIRST_SENDS + AFTER_PAIR + AFTER_NEAR + ((6, 1), (12, 2), (12, 1), (9, 2), (14, 1))
+DELIVERY = (12, 8, 13, 9, 14, 10, 15, 11, 4, 5, 6, 7, 1, 2, 3)
+ALL_SENDS = FIRST_SENDS + AFTER_PAIR + ((1, 2), (8, 1), (8, 2), (6, 1), (12, 2), (12, 1), (9, 2), (14, 1))
 
 
 def flipped(index, offset):
@@ -122,20 +122,37 @@
     return result
 
 
+def as_row(ref):
+    return jnp.concatenate([ref[i : i + 1, :] for i in range(ref.shape[0])], axis=1)
+
+
+def slot_row(owner_row, owners_count, capacity):
+    groups = owner_row.shape[1]
+    numbers = lax.broadcasted_iota(jnp.int32, (owners_count, groups), 0)
+    onehot = numbers == owner_row
+    rows = lax.broadcasted_iota(jnp.int32, (groups, groups), 0)
+    lanes = lax.broadcasted_iota(jnp.int32, (groups, groups), 1)
+    before = (rows < lanes).astype(jnp.bfloat16)
+    earlier = jnp.dot(onehot.astype(jnp.bfloat16), before, preferred_element_type=jnp.float32)
+    position = jnp.sum(jnp.where(onehot, earlier, 0.0), axis=0, keepdims=True)
+    return owner_row * capacity + position.astype(jnp.int32)
+
+
 def sublayer_kernel(
     own_ref,
     gain1_ref,
     shift1_ref,
-    w_ref,
-    segs_col_ref,
-    segs_row_ref,
-    w_out_ref,
+    w_hbm_ref,
+    segments_ref,
+    w_out_hbm_ref,
     gain2_ref,
     shift2_ref,
     w_proj_ref,
     bias_ref,
-    slots_ref,
+    owners_ref,
     out_ref,
+    w_ref,
+    w_out_ref,
     peer_ref,
     normed_ref,
     context_ref,
@@ -146,15 +163,22 @@
     blocks_ref,
     gathered_ref,
     total_ref,
-    far_slots_ref,
+    outgoing_ref,
+    far_owners_ref,
+    segs_col_ref,
+    segs_row_ref,
     send_sems,
     recv_sems,
+    local_sems,
+    give_sems,
+    take_sems,
 ):
     dp, core = lax.axis_index("dp"), lax.axis_index("tensor")
     half, depth = own_ref.shape
     rows = 2 * half
     width = w_ref.shape[1] // 3
     columns = gathered_ref.shape[2]
+    dp_count, _, capacity, _ = outgoing_ref.shape
     score_scale = 1.0 / math.sqrt(width)
     parity = dp // 4 % 2
     beside = (dp, 1 - core)
@@ -186,36 +210,85 @@
         place = gathered_ref.at[flipped(dp, offset)]
         remote(place, place, offset, facing).wait_recv()
 
+    def deliver(offset, pack):
+        source = flipped(dp, 4 * pack)
+        rows_at = pl.ds(pl.multiple_of(source * capacity, capacity), capacity)
+        owner = flipped(dp, offset)
+        target = out_ref.at[rows_at, lanes_of(parity)]
+        if offset == 0:
+            return pltpu.make_async_copy(outgoing_ref.at[dp, pack], target, take_sems.at[0, pack])
+        return pltpu.make_async_remote_copy(
+            src_ref=outgoing_ref.at[owner, pack],
+            dst_ref=target,
+            send_sem=give_sems.at[offset, pack],
+            recv_sem=take_sems.at[offset, pack],
+            device_id=(owner, core),
+            device_id_type=MESH,
+        )
+
+    def wait_delivery(offset, pack):
+        sender = flipped(dp, offset)
+        source = flipped(sender, 4 * pack)
+        rows_at = pl.ds(pl.multiple_of(source * capacity, capacity), capacity)
+        target = out_ref.at[rows_at, lanes_of(sender // 4 % 2)]
+        pltpu.make_async_remote_copy(
+            src_ref=target,
+            dst_ref=target,
+            send_sem=give_sems.at[offset, pack],
+            recv_sem=take_sems.at[offset, pack],
+            device_id=(sender, core),
+            device_id_type=MESH,
+        ).wait_recv()
+
     barrier = pltpu.get_barrier_semaphore()
-    for device in [(flipped(dp, bit), core) for bit in (1, 2, 4, 8)] + [beside]:
+    for device in [(flipped(dp, offset), core) for offset in range(1, dp_count)] + [beside]:
         pl.semaphore_signal(barrier, inc=1, device_id=device, device_id_type=MESH)
-    pl.semaphore_wait(barrier, 5)
+    pl.semaphore_wait(barrier, dp_count)
 
     token_copy = remote(own_ref, peer_ref, 16, beside)
     token_copy.start()
     for send in FIRST_SENDS:
         shard_copy(*send).start()
-    slots_copy = remote(slots_ref, far_slots_ref, 21, facing)
-    slots_copy.start()
+    owners_copy = remote(owners_ref, far_owners_ref, 21, facing)
+    owners_copy.start()
+    w_copy = pltpu.make_async_copy(w_hbm_ref, w_ref, local_sems.at[0])
+    w_copy.start()
+    w_out_copy = pltpu.make_async_copy(w_out_hbm_ref, w_out_ref, local_sems.at[1])
+    w_out_copy.start()
     own_copy = pltpu.make_async_copy(
-        w_proj_ref.at[:, lanes_of(parity)], gathered_ref.at[dp], recv_sems.at[0]
+        w_proj_ref.at[:, lanes_of(parity)], gathered_ref.at[dp], local_sems.at[2]
     )
     own_copy.start()
 
+    groups = segments_ref.shape[1]
+    spread = (
+        lax.broadcasted_iota(jnp.int32, (groups, rows), 0)
+        == lax.shift_right_logical(lax.broadcasted_iota(jnp.int32, (groups, rows), 1), 2)
+    ).astype(jnp.bfloat16)
+    images = jnp.broadcast_to(segments_ref[...].astype(jnp.float32), (128, groups))
+    token_images = jnp.dot(
+        images.astype(jnp.bfloat16), spread, preferred_element_type=jnp.float32
+    )
+    segs_row_ref[...] = token_images[:1]
+    segs_col_ref[...] = token_images.T[:, :1]
+
     step_rows = 128
 
     def first_norm(part, source):
+        gain, shift = as_row(gain1_ref), as_row(shift1_ref)
+
         @pl.loop(0, half // step_rows)
         def _(step):
             at = pl.multiple_of(step * step_rows, step_rows)
             wide = source[pl.ds(at, step_rows), :].astype(jnp.float32)
-            normed = norm_rows(wide, gain1_ref[...], shift1_ref[...])
             to = pl.multiple_of(part * half + step * step_rows, step_rows)
+            normed = norm_rows(wide, gain, shift)
             normed_ref[pl.ds(to, step_rows), :] = normed.astype(jnp.bfloat16)
 
-    first_norm(0, own_ref)
+    first_norm(core, own_ref)
     token_copy.wait_recv()
-    first_norm(1, peer_ref)
+    first_norm(1 - core, peer_ref)
+    w_copy.wait()
 
     chunk = 256
 
@@ -249,32 +322,36 @@
         shard_copy(*send).start()
     heads(3, 6)
     wait_shard(1)
-    wait_shard(8)
-    for send in AFTER_NEAR:
-        shard_copy(*send).start()
-    heads(6, w_ref.shape[0])
+    shard_copy(1, 2).start()
+    heads(6, 7)
     wait_shard(6)
     shard_copy(6, 1).start()
-
-    def terms(first, target):
+    heads(7, w_ref.shape[0])
+
+    def terms(side, target):
         for index in range(half // chunk):
-            lanes = slice(first + index * chunk, first + (index + 1) * chunk)
+            lanes = pl.ds(pl.multiple_of(side * half + index * chunk, chunk), chunk)
             context = context_ref[:, :, lanes].reshape(-1, chunk).T.astype(jnp.bfloat16)
             term = jnp.dot(context, w_out_ref[...], preferred_element_type=jnp.float32)
             target[index * chunk : (index + 1) * chunk, :] = term.astype(jnp.bfloat16)
 
-    terms(half, there_ref)
+    w_out_copy.wait()
+    terms(1 - core, there_ref)
     term_copy = remote(there_ref, arrived_ref, 17, beside)
     term_copy.start()
-    terms(0, here_ref)
+    wait_shard(8)
+    shard_copy(8, 1).start()
+    shard_copy(8, 2).start()
+    terms(core, here_ref)
     term_copy.wait_recv()
+    gain2, shift2 = as_row(gain2_ref), as_row(shift2_ref)
 
     @pl.loop(0, half // step_rows)
     def _(step):
         at = pl.ds(pl.multiple_of(step * step_rows, step_rows), step_rows)
         attn = here_ref[at, :].astype(jnp.float32) + arrived_ref[at, :].astype(jnp.float32)
         hidden = (own_ref[at, :].astype(jnp.float32) + attn).astype(jnp.bfloat16)
-        normed = norm_rows(hidden.astype(jnp.float32), gain2_ref[...], shift2_ref[...])
+        normed = norm_rows(hidden.astype(jnp.float32), gain2, shift2)
         for piece in range(depth // 128):
             pieces_ref[piece] = normed[:, piece * 128 : (piece + 1) * 128]
         quarter = step_rows // 4
@@ -296,9 +373,23 @@
         place = flipped(dp, offset) // 4
         weights = gathered_ref[pl.ds(4 * place, 4)].reshape(-1, columns)
         for block in (first, first + 1):
-            at = slice(block * block_rows, (block + 1) * block_rows)
+            part = core if block == first else 1 - core
+            at = pl.ds(pl.multiple_of((first + part) * block_rows, block_rows), block_rows)
             product = jnp.dot(blocks_ref[block, place], weights, preferred_element_type=jnp.float32)
             total_ref[at, :] = product if fresh else total_ref[at, :] + product
+
+    biases = as_row(bias_ref)
+    bias = jnp.where(parity == 0, biases[:, :columns], biases[:, columns:])
+    places = lax.broadcasted_iota(jnp.int32, (dp_count * capacity, groups), 0)
+
+    def send_pack(pack, owner_row):
+        at = slice(2 * pack * block_rows, 2 * (pack + 1) * block_rows)
+        projected = (total_ref[at, :] + bias).astype(jnp.bfloat16)
+        table = (places == slot_row(owner_row, dp_count, capacity)).astype(jnp.bfloat16)
+        placed = jnp.dot(table, projected, preferred_element_type=jnp.float32)
+        outgoing_ref[:, pack] = placed.astype(jnp.bfloat16).reshape(dp_count, capacity, columns)
+        for offset in DELIVERY + (0,):
+            deliver(offset, pack).start()
 
     wait_shard(12)
     shard_copy(12, 2).start()
@@ -328,29 +419,20 @@
     wait_shard(13)
     wait_shard(15)
     project(12, 0, False)
+    send_pack(0, owners_ref[...])
     project(12, 2, False)
-    slots_copy.wait_recv()
-
-    dp_count, _, capacity, _ = out_ref.shape
-    places = lax.broadcasted_iota(jnp.int32, (dp_count * capacity, 2 * block_rows), 0)
-    for pack, slots in enumerate((slots_ref, far_slots_ref)):
-        at = slice(2 * pack * block_rows, 2 * (pack + 1) * block_rows)
-        projected = (total_ref[at, :] + bias_ref[...]).astype(jnp.bfloat16)
-        table = (places == slots[...]).astype(jnp.bfloat16)
-        placed = jnp.dot(table, projected, preferred_element_type=jnp.float32)
-        slot = parity if pack == 0 else 1 - parity
-        out_ref[:, slot] = placed.astype(jnp.bfloat16).reshape(dp_count, capacity, columns)
+    owners_copy.wait_recv()
+    send_pack(1, far_owners_ref[...])
 
     for send in ALL_SENDS:
         shard_copy(*send).wait_send()
-    for copy in (token_copy, slots_copy, term_copy, far_copy, near_copy, across_copy):
+    for copy in (token_copy, owners_copy, term_copy, far_copy, near_copy, across_copy):
         copy.wait_send()
-
-
-def slot_numbers(dests, dp_count, capacity):
-    onehot = (dests[:, None] == jnp.arange(dp_count, dtype=jnp.int32)[None, :]).astype(jnp.int32)
-    earlier = jnp.cumsum(onehot, axis=0) - onehot
-    return dests * capacity + jnp.sum(earlier * onehot, axis=1)
+    for pack in range(2):
+        deliver(0, pack).wait()
+        for offset in DELIVERY:
+            wait_delivery(offset, pack)
+            deliver(offset, pack).wait_send()
 
 
 def paired_shards(
@@ -367,23 +449,24 @@
     owners,
 ):
     dp_count = lax.axis_size("dp")
-    core = lax.axis_index("tensor")
-    parity = lax.axis_index("dp") // 4 % 2
     columns = w_proj.shape[1] // 2
     half, depth = tokens.shape
     groups = 2 * half // 4
     capacity = 2 * groups // dp_count
-    bias = lax.dynamic_slice_in_dim(proj_bias, parity * columns, columns)
-    token_segs = jnp.repeat(jnp.roll(segments[0], -core * (groups // 2)), 4)
-    slots = jnp.roll(slot_numbers(owners[:, 0], dp_count, capacity), -core * (groups // 2))
     heads_here, width, _ = w_out.shape
+    w_heads = w_qkv.transpose(1, 2, 0)
+    w_out_rows = w_out.reshape(-1, depth)
     half_rows = pltpu.VMEM((half, depth), jnp.bfloat16)
-    outgoing = pl.pallas_call(
+    near = pl.BlockSpec(memory_space=pltpu.VMEM)
+    away = pl.BlockSpec(memory_space=pl.ANY)
+    return pl.pallas_call(
         sublayer_kernel,
-        in_specs=[pl.BlockSpec(memory_space=pltpu.VMEM)] * 12,
-        out_specs=pl.BlockSpec(memory_space=pltpu.VMEM),
-        out_shape=jax.ShapeDtypeStruct((dp_count, 2, capacity, columns), jnp.bfloat16),
+        in_specs=[near, near, near, away, near, away, near, near, away, near, near],
+        out_specs=near,
+        out_shape=jax.ShapeDtypeStruct((dp_count * capacity, 2 * columns), jnp.bfloat16),
         scratch_shapes=[
+            pltpu.VMEM(w_heads.shape, jnp.bfloat16),
+            pltpu.VMEM(w_out_rows.shape, jnp.bfloat16),
             half_rows,
             pltpu.VMEM((2 * half, depth), jnp.bfloat16),
             pltpu.VMEM((heads_here, width, 2 * half), jnp.float32),
@@ -394,9 +477,15 @@
             pltpu.VMEM((4, 4, half // 4, depth), jnp.bfloat16),
             pltpu.VMEM((dp_count, w_proj.shape[0], columns), jnp.bfloat16),
             pltpu.VMEM((half, columns), jnp.float32),
+            pltpu.VMEM((dp_count, 2, capacity, columns), jnp.bfloat16),
             pltpu.VMEM((1, groups), jnp.int32),
+            pltpu.VMEM((2 * half, 1), jnp.float32),
+            pltpu.VMEM((1, 2 * half), jnp.float32),
             pltpu.SemaphoreType.DMA((22,)),
             pltpu.SemaphoreType.DMA((22,)),
+            pltpu.SemaphoreType.DMA((3,)),
+            pltpu.SemaphoreType.DMA((dp_count, 2)),
+            pltpu.SemaphoreType.DMA((dp_count, 2)),
         ],
         compiler_params=pltpu.CompilerParams(
             collective_id=0, has_side_effects=True, vmem_limit_bytes=60 * 2**20
@@ -404,21 +493,17 @@
         cost_estimate=pl.CostEstimate(flops=10**10, bytes_accessed=10**7, transcendentals=0),
     )(
         tokens,
-        ln1_gain[None],
-        ln1_shift[None],
-        w_qkv.transpose(1, 2, 0),
-        token_segs[:, None],
-        token_segs[None],
-        w_out.reshape(-1, depth),
-        ln2_gain[None],
-        ln2_shift[None],
+        ln1_gain.reshape(-1, 128),
+        ln1_shift.reshape(-1, 128),
+        w_heads,
+        segments,
+        w_out_rows,
+        ln2_gain.reshape(-1, 128),
+        ln2_shift.reshape(-1, 128),
         w_proj,
-        bias[None],
-        slots[None],
-    )
-    arrived = lax.all_to_all(outgoing, "dp", split_axis=0, concat_axis=0, tiled=True)
-    arrived = arrived.reshape(dp_count // 8, 2, 4, 2, capacity, columns)
-    return arrived.transpose(0, 3, 2, 4, 1, 5).reshape(dp_count * capacity, 2 * columns)
+        proj_bias.reshape(-1, 128),
+        owners.reshape(1, groups),
+    )
 
 
 def solution(mesh):

time: 177 us -> 149 us (0.84)
  blocking collectives: 47.3 us -> 0 us
  Pallas kernels: 113 us -> 146 us
  local copies, waits for them, and re-layouts: 12.6 us -> 2.85 us
  other arithmetic: 3.52 us -> 0 us
    all_to_all x1 -> x0, blocking collectives: 47.3 us -> none  [paired_shards(): lax.all_to_all(outgoing, 'dp', split_axis=0, concat_axis=0, tiled=True)]
    pallas_call x1, Pallas kernels: 113 us -> 146 us  [paired_shards(): pl.pallas_call(sublayer_kernel, in_specs=[near, near, near, away, near, a...]
    broadcast_in_dim x6 -> x0, local copies, waits for them, and re-layouts: 5.85 us -> none  [the longest x1 1.3 us: paired_shards(): ln1_shift[None]]
    transpose x1 -> x0, local copies, waits for them, and re-layouts: 1.89 us -> none  [paired_shards(): arrived.transpose(0, 3, 2, 4, 1, 5)]
where the time goes in v3:
time: 149 us
  Pallas kernels  146 us (98%)
  local copies, waits for them, and re-layouts  2.85 us (2%)
    pallas_call x1, Pallas kernels, paired_shards(): pl.pallas_call(sublayer_kernel, in_specs=[near, near, near, away, near, a...  146 us

profile of v3, /device:TPU:0, one launch (start us, length us, event | category | flops | bytes accessed | tf_op | source)
XLA Modules:
  0.0 149.1 jit_solution(14935099148095804164)
XLA Ops:
  0.0 146.2 %shard_map.109 = bf16[512,1792]{1,0:T(8,128)(2,1)} custom-call(bf16[512,1408]{1,0:T(8,128)(2,1)} %own_ref.1, f32[11,128]{1,0:T(8,128)} %bitcast.10, f32[11,128]{1,0:T(8,128)} %bitcast.11, bf16[8,264,1408]{2,1,0:T(8,128)(2,1)} %bitcast.8, s32[1,256]{1,0:T(1,128)} %segments_ref.1, bf16[704,1408]{1,0:T(8,128)(2,1)} %bitcast.9, f32[11,128]{1,0:T(8,128)} %bitcast.12, ...), custom_call_target="tpu_custom_call" | custom-call | flops 10000000000 | bytes 10000000 | tf_op jit(solution)/shard_map/pallas_call | solution.py:462
  146.2 2.8 %copy.13 = bf16[512,1792]{1,0:T(8,128)(2,1)} copy(bf16[512,1792]{1,0:T(8,128)(2,1)} %shard_map.109) | data formatting | bytes 3670016
